TPU v7x, 32 devices: a whole 2x2x4 slice. The times are simulated.
32 devices in a mesh: groups: 2 (over y), ctx: 16 (over z, x, core).
Axes of the slice: x: 2, y: 2, z: 4, core: 2. Of those that a mesh axis runs over, the one named last changes fastest.
Arguments:
- queries: bfloat16 [4096, 512], P(('groups', 'ctx')), parts along dimension 0, may hold values from -51 to 51
- keys: bfloat16 [4096, 128], P(('groups', 'ctx')), parts along dimension 0, may hold values from -6 to 6
- values: bfloat16 [4096, 128], P(('groups', 'ctx')), parts along dimension 0, may hold values from -6 to 6
- grad_out: bfloat16 [4096, 512], P(('groups', 'ctx')), parts along dimension 0, may hold values from -24 to 24
- key_blocks: int32 [32, 8], P('groups'), parts along dimension 0, may hold values from 0 to 15, as said below
- key_counts: int32 [32], P('groups'), parts along dimension 0, may hold values from 1 to 8, as said below
- block_slot: int32 [32], P('groups'), parts along dimension 0, may hold values from 0 to 15, each once
Outputs:
- attended: bfloat16 [4096, 512], P(('groups', 'ctx')), parts along dimension 0
- grad_queries: bfloat16 [4096, 512], P(('groups', 'ctx')), parts along dimension 0
- grad_keys: bfloat16 [4096, 128], P(('groups', 'ctx')), parts along dimension 0
- grad_values: bfloat16 [4096, 128], P(('groups', 'ctx')), parts along dimension 0
There are 2 independent parts, one for each index of `groups`. A program takes and returns all parts, laid end to end along the dimension named above; each array names one. Nothing has to cross between parts.
Inputs may be any that keep to these rules, and one draw needn't show every extreme that they name: `key_blocks`: row b: its first key_counts[b] entries are distinct sequence blocks of 0 to b, the first entry being b itself; every later entry equals b. key_counts[b] <= b + 1; the last block's count is 8.
All inputs are finite; a program needn't handle non-finite values.
Results may differ from a plain program's by a relative error of at most 0.017.
Values may be sent and summed in bfloat16 or wider, within the bound.
A program may use at most 128 MiB of HBM per device.

v0:
```python
import math

import jax
import jax.numpy as jnp
from jax import lax
from jax.sharding import PartitionSpec as P

BLK = 128


NEG_LARGE = -1e30


def job_scores(work_item, block_tiles, slot_group, size_pack):
    query_rows, grad_rows, query_block, key_list, stored_list, key_count, low_group, high_group = (
        work_item
    )
    block_rows, head_count, group_size, score_scale = size_pack
    key_tiles, value_tiles = block_tiles
    slot_start = slot_group * group_size
    picked = lax.dynamic_slice_in_dim(stored_list, slot_start, group_size)
    key_rows = jnp.take(key_tiles, picked, axis=0).reshape(
        group_size * block_rows, key_tiles.shape[2]
    )
    value_rows = jnp.take(value_tiles, picked, axis=0).reshape(
        group_size * block_rows, value_tiles.shape[2]
    )
    seq_blocks = lax.dynamic_slice_in_dim(key_list, slot_start, group_size)
    columns = jnp.arange(group_size * block_rows, dtype=jnp.int32)
    slot_of = columns // block_rows
    key_position = jnp.repeat(seq_blocks, block_rows) * block_rows + columns % block_rows
    query_position = (
        query_block * block_rows
        + jnp.arange(block_rows * head_count, dtype=jnp.int32) // head_count
    )
    in_list = slot_start + slot_of < key_count
    allowed = in_list[None, :] & (key_position[None, :] <= query_position[:, None])
    scores = jnp.dot(query_rows, key_rows.T, preferred_element_type=jnp.float32) * score_scale
    return (scores, allowed, key_rows, value_rows)


def softmax_stats(work_item, block_tiles, size_pack):
    row_count = work_item[0].shape[0]

    def softmax_visit_group(slot_group, state_pair):
        running_max, running_sum = state_pair
        scored = job_scores(work_item, block_tiles, slot_group, size_pack)
        masked = jnp.where(scored[1], scored[0], NEG_LARGE)
        new_max = jnp.maximum(running_max, jnp.max(masked, axis=1))
        exp_terms = jnp.where(scored[1], jnp.exp(masked - new_max[:, None]), 0.0)
        return (new_max, running_sum * jnp.exp(running_max - new_max) + jnp.sum(exp_terms, axis=1))

    start_state = (
        jnp.full((row_count,), NEG_LARGE, jnp.float32),
        jnp.zeros((row_count,), jnp.float32),
    )
    return lax.fori_loop(work_item[6], work_item[7], softmax_visit_group, start_state)


def attend_pass(work_item, block_tiles, size_pack, log_total):
    row_count = work_item[0].shape[0]
    head_dim = work_item[0].shape[1]

    def attend_visit_group(slot_group, running_total):
        scores, allowed, key_rows, value_rows = job_scores(
            work_item, block_tiles, slot_group, size_pack
        )
        weights = jnp.where(allowed, jnp.exp(scores - log_total[:, None]), 0.0).astype(jnp.bfloat16)
        return running_total + jnp.dot(weights, value_rows, preferred_element_type=jnp.float32)

    return lax.fori_loop(
        work_item[6],
        work_item[7],
        attend_visit_group,
        jnp.zeros((row_count, head_dim), jnp.float32),
    )


def gradient_pass(work_item, block_tiles, size_pack, log_total, row_delta):
    query_rows, grad_rows = (work_item[0], work_item[1])
    block_rows, head_count, group_size, score_scale = size_pack
    row_count, head_dim = query_rows.shape
    slot_total = work_item[3].shape[0]

    def gradient_visit_group(slot_group, state_pair):
        query_grad_sum, slot_grads = state_pair
        scores, allowed, key_rows, value_rows = job_scores(
            work_item, block_tiles, slot_group, size_pack
        )
        prob_values = jnp.where(allowed, jnp.exp(scores - log_total[:, None]), 0.0)
        dprobs = jnp.dot(grad_rows, value_rows.T, preferred_element_type=jnp.float32)
        dscores = (prob_values * (dprobs - row_delta[:, None])).astype(jnp.bfloat16)
        query_grad_sum = query_grad_sum + jnp.dot(
            dscores, key_rows, preferred_element_type=jnp.float32
        )
        weights = prob_values.astype(jnp.bfloat16)
        key_part = jnp.dot(dscores.T, query_rows, preferred_element_type=jnp.float32) * score_scale
        value_part = jnp.dot(weights.T, grad_rows, preferred_element_type=jnp.float32)
        both_parts = jnp.concatenate([key_part, value_part], axis=1)
        slot_grads = lax.dynamic_update_slice_in_dim(
            slot_grads, both_parts, slot_group * group_size * block_rows, 0
        )
        return (query_grad_sum, slot_grads)

    empty_slots = jnp.zeros((slot_total * block_rows, 2 * head_dim), jnp.float32)
    start_state = (jnp.zeros((row_count, head_dim), jnp.float32), empty_slots)
    return lax.fori_loop(work_item[6], work_item[7], gradient_visit_group, start_state)


def place_tiles(slot_sets, block_count, slot_total, tile_width):
    placed = jnp.zeros((block_count, tile_width), jnp.float32)
    for stored_list, slot_grads in slot_sets:
        target = stored_list
        inside = (target >= 0) & (target < block_count)
        target = jnp.where(inside, target, block_count)
        placed = placed.at[target].add(slot_grads.reshape(slot_total, tile_width), mode="drop")
    return placed


def per_device(queries, keys, values, grad_out, key_blocks, key_counts, block_slot):
    device = lax.axis_index("ctx")
    token_rows, query_width = queries.shape
    head_dim = keys.shape[1]
    head_count = query_width // head_dim
    block_rows = BLK
    local_blocks = token_rows // block_rows
    block_total, slot_total = key_blocks.shape
    group_size = min(16, slot_total)
    score_scale = 1.0 / math.sqrt(head_dim)
    size_pack = (block_rows, head_count, group_size, score_scale)
    tile_width = block_rows * 2 * head_dim
    block_order = jnp.argsort(block_slot)
    gathered = (
        lax.all_gather(keys, "ctx", axis=0, tiled=True),
        lax.all_gather(values, "ctx", axis=0, tiled=True),
    )
    block_tiles = (
        gathered[0].reshape(block_total, block_rows, head_dim),
        gathered[1].reshape(block_total, block_rows, head_dim),
    )
    query_tiles = queries.reshape(local_blocks, block_rows * head_count, head_dim)
    grad_tiles = grad_out.reshape(local_blocks, block_rows * head_count, head_dim)
    query_block = block_order[device * local_blocks + 0]
    key_list = key_blocks[query_block]
    key_count = key_counts[query_block]
    stored_list = jnp.take(block_slot, key_list)
    group_count = (key_count + group_size - 1) // group_size
    low_group = jnp.int32(0)
    own_jobs = [
        (
            query_tiles[0],
            grad_tiles[0],
            query_block,
            key_list,
            stored_list,
            key_count,
            low_group,
            group_count,
        )
    ]
    own_stats = [softmax_stats(work_item, block_tiles, size_pack) for work_item in own_jobs]
    own_log_total = jnp.stack([pair_stat[0] + jnp.log(pair_stat[1]) for pair_stat in own_stats])
    own_out = jnp.stack(
        [
            attend_pass(work_item, block_tiles, size_pack, own_log_total[number])
            for number, work_item in enumerate(own_jobs)
        ]
    )
    attended_tiles = own_out.astype(jnp.bfloat16)
    row_delta = jnp.sum(grad_tiles.astype(jnp.float32) * attended_tiles.astype(jnp.float32), axis=2)
    own_results = [
        gradient_pass(work_item, block_tiles, size_pack, own_log_total[number], row_delta[number])
        for number, work_item in enumerate(own_jobs)
    ]
    query_grad_sum = jnp.stack([pass_result[0] for pass_result in own_results])
    slot_sets = [
        (work_item[4], pass_result[1]) for work_item, pass_result in zip(own_jobs, own_results)
    ]
    attended = attended_tiles.reshape(token_rows, query_width)
    grad_queries = (
        (query_grad_sum * score_scale).astype(jnp.bfloat16).reshape(token_rows, query_width)
    )
    row_count = token_rows * lax.axis_size("ctx")
    placed = place_tiles(slot_sets, row_count // block_rows, slot_total, tile_width)
    grad_rows_all = lax.psum_scatter(
        placed.reshape(row_count, 2 * head_dim), "ctx", scatter_dimension=0, tiled=True
    )
    grad_keys = grad_rows_all[:, :head_dim].astype(jnp.bfloat16)
    grad_values = grad_rows_all[:, head_dim:].astype(jnp.bfloat16)
    return (attended, grad_queries, grad_keys, grad_values)


def solution(mesh):
    placed = (
        P(("groups", "ctx"), None),
        P(("groups", "ctx"), None),
        P(("groups", "ctx"), None),
        P(("groups", "ctx"), None),
        P("groups", None),
        P("groups"),
        P("groups"),
    )
    return jax.shard_map(
        per_device,
        mesh=mesh,
        in_specs=placed,
        out_specs=(
            P(("groups", "ctx"), None),
            P(("groups", "ctx"), None),
            P(("groups", "ctx"), None),
            P(("groups", "ctx"), None),
        ),
        check_vma=False,
    )
```

profile of v0, /device:TPU:0, one launch (start us, length us, event | category | flops | bytes accessed | tf_op | source)
XLA Modules:
  0.0 146.3 jit_solution(10967985898112311635)
XLA Ops:
  7.2 0.0 copy-start
  7.2 0.0 copy-start.2
  7.2 0.0 reduce-scatter.2.cloned.1.call-start
  7.3 1.9 %sort.17 = (s32[16]{0:T(128)}, s32[16]{0:T(128)S(1)}) sort(s32[16]{0:T(128)} %param.21, s32[16]{0:T(128)S(1)} %iota.84), dimensions={0}, to_apply=%region_0.0 | sort | flops 64 | bytes 256 | tf_op jit(solution)/shard_map/jit(argsort)/sort | solution.py:132
  9.1 0.6 dynamic_slice.12
  11.7 1.2 dynamic_slice.18
  13.6 0.0 copy-done
  13.6 0.2 dynamic-slice_reduce_fusion
  13.8 1.3 gather_fusion
  15.1 1.0 squeeze_reshape.7
  16.8 24.8 %all_gather.7 = bf16[2048,128]{1,0:T(8,128)(2,1)S(1)} all-gather(bf16[128,128]{1,0:T(8,128)(2,1)} %param.17), channel_id=1, replica_groups=mesh['groups'=2,'ctx'=16] {'ctx'}, dimensions={0}, use_global_device_ids=true | all-gather | bytes 557056 | tf_op jit(solution)/shard_map/all_gather | solution.py:135
  41.6 19.1 %all_gather.6 = bf16[2048,128]{1,0:T(8,128)(2,1)S(1)} all-gather(bf16[128,128]{1,0:T(8,128)(2,1)} %param.16), channel_id=1, replica_groups=mesh['groups'=2,'ctx'=16] {'ctx'}, dimensions={0}, use_global_device_ids=true | all-gather | bytes 557056 | tf_op jit(solution)/shard_map/all_gather | solution.py:134
  60.7 0.6 gather_fusion.2
  61.3 0.6 gather_fusion.1
  61.9 0.0 copy-done.2
  61.9 0.1 squeeze_reshape.6
  62.0 0.1 broadcast_select_fusion
  62.2 2.3 %while.44 = (s32[]{:T(128)}, f32[512]{0:T(512)S(1)}, f32[512]{0:T(512)S(1)}, s32[]{:T(128)}, s32[]{:T(128)}, /*index=5*/s32[8]{0:T(128)S(1)}, s32[]{:T(128)}, bf...) while((s32[]{:T(128)}, f32[512]{0:T(512)S(1)}, ...), condition=%wide.region_4.6_spmd, body=%wide.region_1.5_spmd.sunk | while | flops 139483664 | bytes 4635885 | solution.py:57
  62.2 0.1 fusion.104
  62.3 0.7 fusion.105
  62.9 0.7 fusion.106
  63.7 0.8 select_reduce_fusion.2
  64.5 1.7 %while.45 = (s32[]{:T(128)}, f32[512,128]{1,0:T(8,128)S(1)}, s32[]{:T(128)}, s32[]{:T(128)}, s32[8]{0:T(128)S(1)}, /*index=5*/s32[]{:T(128)}, bf16[8,128,128]{2,...) while((s32[]{:T(128)}, f32[512,128]{1,0:T(8,128)S(1)}, ...), condition=%wide.region_6.8_spmd, body=%wide.region_5.7_spmd.sunk | while | flops 271668736 | bytes 1196277 | solution.py:71
  64.6 0.1 fusion.110
  64.6 0.7 fusion.112
  65.3 0.9 fusion.113
  66.3 0.7 multiply_reduce_fusion
  67.0 1.1 broadcast_in_dim.95
  68.1 4.2 %while.46 = (s32[]{:T(128)}, f32[512,128]{1,0:T(8,128)S(1)}, f32[1024,256]{0,1:T(8,128)}, s32[]{:T(128)}, s32[]{:T(128)}, /*index=5*/s32[8]{0:T(128)S(1)}, s32[]...) while((s32[]{:T(128)}, f32[512,128]{1,0:T(8,128)S(1)}, ...), condition=%wide.region_9.11_spmd, body=%wide.region_8.10_spmd.sunk | while | flops 676288000 | bytes 14436621 | solution.py:107
  68.1 0.1 fusion.124
  68.2 0.7 fusion.126
  68.8 0.8 exponential_select_fusion.2
  69.6 0.4 multiply_convert_fusion.3
  70.1 0.4 convolution_add_fusion.2
  70.5 0.4 fusion.127
  70.9 0.4 convolution_multiply_fusion.2
  71.2 1.1 pad_maximum_fusion.2
  72.3 1.6 %copy.11 = f32[1024,256]{1,0:T(8,128)S(1)} copy(f32[1024,256]{0,1:T(8,128)} %get-tuple-element.628) | data formatting | bytes 2097152 | tf_op jit(solution)/shard_map/while | solution.py:107
  73.9 0.2 reshape.351
  74.1 2.2 %scatter_custom_fusion = f32[16,32768]{1,0:T(8,128)S(1)} fusion(s32[8]{0:T(128)S(1)} %fusion.56, f32[8,32768]{1,0:T(8,128)S(1)} %reshape.351, f32[]{:T(128)} %constant.366.clone.1), kind=kCustom, calls=%fused_computation.95 | custom fusion | flops 262144 | bytes 2097156 | tf_op jit(solution)/shard_map/scatter-add | solution.py:116
  76.3 1.5 %reshape.322 = f32[2048,256]{1,0:T(8,128)} reshape(f32[16,32768]{1,0:T(8,128)S(1)} %scatter_custom_fusion) | data formatting | bytes 4194304 | tf_op jit(solution)/shard_map/reshape | solution.py:186
  77.8 0.0 reduce-scatter.2.cloned.1.call-update
  77.8 0.9 copy-done.1
  78.7 0.7 reshape.319
  79.5 0.7 reshape.320
  80.2 57.7 %reduce-scatter.2.cloned.1.call-done = f32[128,256]{1,0:T(8,128)} async-done(((f32[2048,256]{1,0:T(8,128)}), f32[128,256]{1,0:T(8,128)}) %reduce-scatter.2.cloned.1.call-update) | async-done | bytes 131088 | tf_op jit(solution)/shard_map/reduce_scatter | solution.py:185
  138.0 0.9 convert.4
  138.9 0.6 fusion.59
  (22 shorter events, 0.2 us)
Async XLA Ops:
  7.2 6.4 %copy-start = (s32[16,8]{0,1:T(8,128)S(1)}, s32[16,8]{0,1:T(8,128)}, u32[]{:S(2)}) copy-start(s32[16,8]{0,1:T(8,128)} %param.19) | copy-start | bytes 1540
  7.2 54.7 %copy-start.2 = (bf16[128,512]{1,0:T(8,128)(2,1)S(1)}, bf16[128,512]{1,0:T(8,128)(2,1)}, u32[]{:S(2)}) copy-start(bf16[128,512]{1,0:T(8,128)(2,1)} %param.15) | copy-start | bytes 393220
  7.2 130.8 %reduce-scatter.2.cloned.1.call-start = ((), (), s32[]{:S(2)}) async-start(), calls=%async_computation.1 | async-start | bytes 2228224 | tf_op jit(solution)/shard_map/reduce_scatter | solution.py:185
  77.8 0.9 copy-start.1
Sparse Core Ops, SparseCore 0:
  78.0 59.9 reduce-scatter.1
where the time goes:
time: 147 us; the launch traced here: 146 us
  waiting for transfers between devices  57.7 us (39%)
  blocking collectives  43.9 us (30%)
  between operations  17.5 us (12%)
  local copies, waits for them, and re-layouts  13 us (9%)
  other arithmetic  9.98 us (7%)
  matrix products  4.03 us (3%)
    reduce_scatter x1, waiting for transfers between devices, per_device(): lax.psum_scatter(placed.reshape(row_count, 2 * head_dim), 'ctx', scatter_...  57.7 us
    all_gather x1, blocking collectives, per_device(): lax.all_gather(values, 'ctx', axis=0, tiled=True)  24.8 us
    all_gather x1, blocking collectives, per_device(): lax.all_gather(keys, 'ctx', axis=0, tiled=True)  19.1 us
  transfers between devices with their start and end apart: 1, of which 1 were waited for; matrix products, arithmetic and copies ran while one was open for 1% of the time, Pallas kernels for 0%

commit v1 on v0

v1 whole, which is shorter than its diff:
```python
import functools
import math

import jax
import jax.numpy as jnp
from jax import lax
from jax.experimental import pallas as pl
from jax.experimental.pallas import tpu as pltpu
from jax.sharding import PartitionSpec as P

BLK = 128
NEG = -1e30
F32 = jnp.float32
BF16 = jnp.bfloat16
MESH = pl.DeviceIdType.MESH


def grid_of(device_total):
    chips = device_total // 2
    power = chips.bit_length() - 1
    x_size = 2 ** (power // 3)
    return chips // x_size, x_size


def loop(count, body, most=4):
    if count <= most:
        for step in range(count):
            body(step)
    else:
        lax.fori_loop(0, count, lambda step, _: (body(step), 0)[1], 0)


def dot(a, b, a_dim, b_dim):
    return lax.dot_general(a, b, (((a_dim,), (b_dim,)), ((), ())), preferred_element_type=F32)


def kernel(
    sizes,
    q_ref, k_ref, v_ref, g_ref, lists_ref, counts_ref, slot_ref,
    out_ref, dq_ref, dk_ref, dv_ref,
    kv, q_rows, g_rows, q_cols, g_cols, bias, tri, top, total, acc, dq_acc, tops,
    exps, dprobs, part, from_core, from_x, from_z,
    ag_send, ag_recv, rs_send, rs_recv,
):
    heads, head_dim, z_size, x_size, keep = sizes
    device_total = 2 * x_size * z_size
    lines = 2 * x_size
    rows = heads * BLK
    scale = 1.0 / math.sqrt(head_dim)
    scale2 = scale * math.log2(math.e)
    me = lax.axis_index("ctx")
    group = lax.axis_index("groups")
    c = lax.rem(me, 2)
    x = lax.rem(me // 2, x_size)
    z = me // (2 * x_size)
    other = 1 - c

    def device(zi, xi, ci):
        return (group, (zi * x_size + xi) * 2 + ci)

    def place(z_step, x_step, c_step):
        return (x_step * 2 + c_step) * z_size + z_step

    def tile(block):
        return pl.ds(pl.multiple_of(block * BLK, BLK), BLK)

    def turn_z(step):
        return lax.rem(z + step, z_size)

    def turn_x(step):
        return lax.rem(x + step, x_size)

    mine = 0
    kv[mine, 0] = k_ref[...]
    kv[mine, 1] = v_ref[...]
    barrier = pltpu.get_barrier_semaphore()
    for step in range(1, z_size):
        pl.semaphore_signal(barrier, inc=1, device_id=device(turn_z(step), x, c), device_id_type=MESH)
    for step in range(1, x_size):
        pl.semaphore_signal(barrier, inc=1, device_id=device(z, turn_x(step), c), device_id_type=MESH)
    pl.semaphore_signal(barrier, inc=1, device_id=device(z, x, other), device_id_type=MESH)

    pl.semaphore_wait(barrier, z_size + x_size - 1)

    def share(block, there, where, number):
        return pltpu.make_async_remote_copy(
            src_ref=kv.at[block],
            dst_ref=kv.at[there],
            send_sem=ag_send.at[number],
            recv_sem=ag_recv.at[there],
            device_id=where,
            device_id_type=MESH,
        )

    x_base = z_size - 1
    core_base = x_base + (x_size - 1) * z_size

    def share_z(step):
        return share(mine, place(z_size - step, 0, 0), device(turn_z(step), x, c), step - 1)

    def share_x(x_step, z_step):
        return share(
            place(z_step, 0, 0),
            place(z_step, x_size - x_step, 0),
            device(z, turn_x(x_step), c),
            x_base + (x_step - 1) * z_size + z_step,
        )

    def share_core(x_step, z_step):
        return share(
            place(z_step, x_step, 0),
            place(z_step, x_step, 1),
            device(z, x, other),
            core_base + x_step * z_size + z_step,
        )

    loop(z_size - 1, lambda i: share_z(i + 1).start(), 15)
    loop(x_size - 1, lambda i: share_x(i + 1, 0).start())
    share_core(0, 0).start()

    for h in range(heads):
        cols = slice(h * head_dim, (h + 1) * head_dim)
        q_tile = q_ref[:, cols]
        g_tile = g_ref[:, cols]
        q_rows[h * BLK:(h + 1) * BLK, :] = q_tile
        g_rows[h * BLK:(h + 1) * BLK, :] = g_tile
        q_cols[:, h * BLK:(h + 1) * BLK] = q_tile.T
        g_cols[:, h * BLK:(h + 1) * BLK] = g_tile.T

    block_total, slot_total = lists_ref.shape

    def find(j, found):
        return jnp.where(slot_ref[j] == me, j, found)

    query_block = lax.fori_loop(0, block_total, find, jnp.int32(0))
    count = counts_ref[query_block]
    bias[...] = jnp.full(bias.shape, NEG, F32)
    block_ids = lax.broadcasted_iota(jnp.int32, bias.shape, 0)

    def open_block(k, _):
        stored = slot_ref[lists_ref[query_block, k]]
        c_step = lax.rem(stored + c, 2)
        x_step = lax.rem(stored // 2 - x + lines, x_size)
        z_step = lax.rem(stored // lines - z + z_size, z_size)
        spot = place(z_step, x_step, c_step)
        spot = jnp.where(k < count, spot, -1)
        bias[...] = jnp.where(block_ids == spot, 0.0, bias[...])
        return 0

    lax.fori_loop(0, slot_total, open_block, 0)
    key_at = lax.broadcasted_iota(jnp.int32, (BLK, rows), 0)
    query_at = lax.rem(lax.broadcasted_iota(jnp.int32, (BLK, rows), 1), BLK)
    tri[...] = jnp.where(key_at <= query_at, 0.0, NEG)
    top[...] = jnp.full(top.shape, NEG, F32)
    total[...] = jnp.zeros(total.shape, F32)
    acc[...] = jnp.zeros(acc.shape, F32)
    dq_acc[...] = jnp.zeros(dq_acc.shape, F32)

    def scores_of(block, own):
        raw = dot(kv[block, 0], q_cols[...], 1, 0) * scale2
        return raw + (tri[...] if own else bias[pl.ds(block, 1), :])

    def forward(block, own=False):
        values = kv[block, 1]
        scores = scores_of(block, own)
        old = top[...]
        new = jnp.maximum(old, jnp.max(scores, axis=0, keepdims=True))
        terms = jnp.exp2(scores - new)
        fade = jnp.exp2(old - new)
        top[...] = new
        total[...] = total[...] * fade + jnp.sum(terms, axis=0, keepdims=True)
        acc[...] = acc[...] * fade + dot(values, terms.astype(BF16), 0, 0)
        if keep:
            exps[tile(block), :] = terms
            tops[pl.ds(block, 1), :] = new
            dprobs[tile(block), :] = dot(values, g_cols[...], 1, 0)

    forward(mine, True)

    def take_z(i):
        step = i + 1
        block = place(step, 0, 0)
        share(mine, block, device(z, x, other), 0).wait_recv()
        loop(x_size - 1, lambda j: share_x(j + 1, step).start())
        share_core(0, step).start()

    loop(z_size - 1, take_z)
    loop(z_size - 1, lambda i: forward(place(i + 1, 0, 0)), 0)

    def take_x(x_step):
        def one(step):
            block = place(step, x_step, 0)
            share(mine, block, device(z, x, other), 0).wait_recv()
            share_core(x_step, step).start()

        loop(z_size, one)
        loop(z_size, lambda step: forward(place(step, x_step, 0)), 0)

    loop(x_size - 1, lambda i: take_x(i + 1))

    def take_core(x_step):
        def one(step):
            block = place(step, x_step, 1)
            share(mine, block, device(z, x, other), 0).wait_recv()
            forward(block)

        loop(z_size, one, 0)

    loop(x_size, take_core, 0)

    inverse = 1.0 / total[...]
    attended = (acc[...] * inverse).T.astype(BF16)
    for h in range(heads):
        part_rows = slice(h * BLK, (h + 1) * BLK)
        out_ref[:, h * head_dim:(h + 1) * head_dim] = attended[part_rows, :]
    rounded = (acc[...] * inverse).astype(BF16).astype(F32)
    delta = jnp.sum(g_cols[...].astype(F32) * rounded, axis=0, keepdims=True)
    total[...] = inverse
    acc[0:1, :] = delta

    def backward(block, own=False):
        keys = kv[block, 0]
        if keep:
            probs = exps[tile(block), :] * (
                jnp.exp2(tops[pl.ds(block, 1), :] - top[...]) * total[...]
            )
            dprob = dprobs[tile(block), :]
        else:
            probs = jnp.exp2(scores_of(block, own) - top[...]) * total[...]
            dprob = dot(kv[block, 1], g_cols[...], 1, 0)
        dscores = (probs * (dprob - acc[0:1, :])).astype(BF16)
        dq_acc[...] += dot(keys, dscores, 0, 0)
        dkey = dot(dscores, q_rows[...], 1, 0) * scale
        dvalue = dot(probs.astype(BF16), g_rows[...], 1, 0)
        return dkey, dvalue

    def post(block, pair):
        part[block, 0] = pair[0].astype(BF16)
        part[block, 1] = pair[1].astype(BF16)

    def plus(pair, landed, slot):
        return (
            pair[0] + landed[slot, 0].astype(F32),
            pair[1] + landed[slot, 1].astype(F32),
        )

    def give(block, landed, slot, where, number):
        return pltpu.make_async_remote_copy(
            src_ref=part.at[block],
            dst_ref=landed.at[slot],
            send_sem=rs_send.at[number],
            recv_sem=rs_recv.at[number],
            device_id=where,
            device_id_type=MESH,
        )

    def give_core(x_at, z_at):
        slot = x_at * z_size + z_at
        return give(
            place(z_at, x_at, 1), from_core, slot, device(z, x, other), core_base + slot
        )

    def give_x(x_step, z_at):
        slot = (x_step - 1) * z_size + z_at
        return give(
            place(z_at, x_step, 0), from_x, slot, device(z, turn_x(x_step), c), x_base + slot
        )

    def give_z(z_step):
        return give(
            place(z_step, 0, 0), from_z, z_step - 1, device(turn_z(z_step), x, c), z_step - 1
        )

    def to_core(x_at):
        def one(z_at):
            block = place(z_at, x_at, 1)
            post(block, backward(block))
            give_core(x_at, z_at).start()

        loop(z_size, one, 0)

    def to_x(x_step):
        x_at = x_step

        def one(i):
            z_at = lax.rem(i + 1, z_size)
            block = place(z_at, x_at, 0)
            pair = backward(block)
            give_core(x_at, z_at).wait_recv()
            post(block, plus(pair, from_core, x_at * z_size + z_at))
            give_x(x_step, z_at).start()

        loop(z_size, one, 0)

    def away(i):
        to_core(i + 1)
        to_x(i + 1)

    loop(x_size - 1, away, 1)
    to_core(0)

    def gathered(z_at, own):
        block = place(z_at, 0, 0)
        pair = backward(block, own)
        give_core(0, z_at).wait_recv()
        pair = plus(pair, from_core, z_at)
        for x_step in range(1, x_size):
            give_x(x_step, z_at).wait_recv()
            pair = plus(pair, from_x, (x_step - 1) * z_size + z_at)
        return block, pair

    def to_z(i):
        block, pair = gathered(i + 1, False)
        post(block, pair)
        give_z(i + 1).start()

    loop(z_size - 1, to_z, 0)
    block, pair = gathered(0, True)
    query_grad = (dq_acc[...] * scale).T.astype(BF16)
    for h in range(heads):
        dq_ref[:, h * head_dim:(h + 1) * head_dim] = query_grad[h * BLK:(h + 1) * BLK, :]
    for z_step in range(1, z_size):
        give_z(z_step).wait_recv()
        pair = plus(pair, from_z, z_step - 1)
    dk_ref[...] = pair[0].astype(BF16)
    dv_ref[...] = pair[1].astype(BF16)

    loop(device_total - 1, lambda i: share(mine, mine, device(z, x, other), i).wait_send(), 0)
    loop(
        device_total - 1,
        lambda i: give(mine, from_core, 0, device(z, x, other), i).wait_send(),
        0,
    )


def per_device(queries, keys, values, grad_out, key_blocks, key_counts, block_slot):
    token_rows, width = queries.shape
    head_dim = keys.shape[1]
    heads = width // head_dim
    device_total = key_blocks.shape[0] * BLK // token_rows
    z_size, x_size = grid_of(device_total)
    keep = device_total <= 32
    rows = heads * BLK
    kept = device_total * BLK if keep else 8
    vmem = pl.BlockSpec(memory_space=pltpu.VMEM)
    smem = pl.BlockSpec(memory_space=pltpu.SMEM)
    call = pl.pallas_call(
        functools.partial(kernel, (heads, head_dim, z_size, x_size, keep)),
        out_shape=(
            jax.ShapeDtypeStruct(queries.shape, BF16),
            jax.ShapeDtypeStruct(queries.shape, BF16),
            jax.ShapeDtypeStruct(keys.shape, BF16),
            jax.ShapeDtypeStruct(values.shape, BF16),
        ),
        in_specs=[vmem] * 4 + [smem] * 3,
        out_specs=(vmem,) * 4,
        scratch_shapes=[
            pltpu.VMEM((device_total, 2, BLK, head_dim), BF16),
            pltpu.VMEM((rows, head_dim), BF16),
            pltpu.VMEM((rows, head_dim), BF16),
            pltpu.VMEM((head_dim, rows), BF16),
            pltpu.VMEM((head_dim, rows), BF16),
            pltpu.VMEM((device_total, rows), F32),
            pltpu.VMEM((BLK, rows), F32),
            pltpu.VMEM((1, rows), F32),
            pltpu.VMEM((1, rows), F32),
            pltpu.VMEM((head_dim, rows), F32),
            pltpu.VMEM((head_dim, rows), F32),
            pltpu.VMEM((device_total, rows), F32),
            pltpu.VMEM((kept, rows), F32),
            pltpu.VMEM((kept, rows), F32),
            pltpu.VMEM((device_total, 2, BLK, head_dim), BF16),
            pltpu.VMEM((x_size * z_size, 2, BLK, head_dim), BF16),
            pltpu.VMEM((max(1, (x_size - 1) * z_size), 2, BLK, head_dim), BF16),
            pltpu.VMEM((max(1, z_size - 1), 2, BLK, head_dim), BF16),
            pltpu.SemaphoreType.DMA((device_total,)),
            pltpu.SemaphoreType.DMA((device_total,)),
            pltpu.SemaphoreType.DMA((device_total,)),
            pltpu.SemaphoreType.DMA((device_total,)),
        ],
        compiler_params=pltpu.CompilerParams(
            collective_id=0, has_side_effects=True, vmem_limit_bytes=48 * 1024 * 1024
        ),
        name="sparse_attention",
    )
    return call(queries, keys, values, grad_out, key_blocks, key_counts, block_slot)


def solution(mesh):
    wide = P(("groups", "ctx"), None)
    return jax.shard_map(
        per_device,
        mesh=mesh,
        in_specs=(wide, wide, wide, wide, P("groups", None), P("groups"), P("groups")),
        out_specs=(wide,) * 4,
        check_vma=False,
    )
```

time: 147 us -> 43.2 us (0.29)
  waiting for transfers between devices: 57.7 us -> 0 us
  blocking collectives: 43.9 us -> 0 us
  Pallas kernels: 0 us -> 35.6 us
  between operations: 17.5 us -> 0.66 us
  other arithmetic: 9.98 us -> 0 us
  local copies, waits for them, and re-layouts: 13 us -> 6.64 us
  matrix products: 4.03 us -> 0 us
    reduce_scatter x1 -> x0, waiting for transfers between devices: 57.7 us -> none  [per_device(): lax.psum_scatter(placed.reshape(row_count, 2 * head_dim), 'ctx', scatter_...]
    all_gather x2 -> x0, blocking collectives: 43.9 us -> none  [the longest x1 24.8 us: per_device(): lax.all_gather(values, 'ctx', axis=0, tiled=True)]
    pallas_call x0 -> x1, Pallas kernels: none -> 35.6 us  [per_device(): call(queries, keys, values, grad_out, key_blocks, key_counts, block_slot)]
    unnamed x6 -> x17, local copies, waits for them, and re-layouts: 0.89 us -> 6.64 us
    dot_general x7 -> x0, matrix products: 4.03 us -> none  [the longest x2 1.47 us: job_scores(): jnp.dot(query_rows, key_rows.T, preferred_element_type=jnp.float32)]
    reshape x4 -> x0, local copies, waits for them, and re-layouts: 3.2 us -> none  [the longest x1 1.53 us: per_device(): placed.reshape(row_count, 2 * head_dim)]
    gather x3 -> x0, local copies, waits for them, and re-layouts: 2.49 us -> none  [the longest x1 1.3 us: per_device(): stored_list = jnp.take(block_slot, key_list)]
    scatter-add x1 -> x0, other arithmetic: 2.2 us -> none  [place_tiles(): placed.at[target]]
  transfers between devices with their start and end apart: 1 -> 0, of which waited for: 1 -> 0; matrix products, arithmetic and copies ran while one was open for 1% -> 0% of each run, Pallas kernels for 0% -> 0%
where the time goes in v1:
time: 43.2 us; the launch traced here: 42.9 us
  Pallas kernels  35.6 us (82%)
  local copies, waits for them, and re-layouts  6.64 us (15%)
  between operations  0.66 us (2%)
    pallas_call x1, Pallas kernels, per_device(): call(queries, keys, values, grad_out, key_blocks, key_counts, block_slot)  35.6 us
    unnamed x17, local copies, waits for them, and re-layouts  6.64 us

profile of v1, /device:TPU:0, one launch (start us, length us, event | category | flops | bytes accessed | tf_op | source)
XLA Modules:
  0.0 42.9 jit_solution(7855701649536307207)
XLA Ops:
  0.6 0.0 copy-start.5
  0.6 0.0 copy-start.4
  0.7 0.8 %copy.11.lists_ref = s32[16,8]{1,0:T(8,128)S(1)} copy(s32[16,8]{0,1:T(8,128)} %param.11) | data formatting | bytes 1024 | tf_op args[4]
  1.4 0.0 copy-done.5
  1.4 0.0 copy-done.4
  1.4 0.0 copy-start
  1.4 0.9 %copy-done = bf16[128,512]{1,0:T(8,128)(2,1)S(1)} copy-done((bf16[128,512]{1,0:T(8,128)(2,1)S(1)}, bf16[128,512]{1,0:T(8,128)(2,1)}, u32[]{:S(2)}) %copy-start) | copy-done | bytes 131096
  2.3 0.0 copy-start.1
  2.3 0.9 %copy-done.1 = bf16[128,512]{1,0:T(8,128)(2,1)S(1)} copy-done((bf16[128,512]{1,0:T(8,128)(2,1)S(1)}, bf16[128,512]{1,0:T(8,128)(2,1)}, u32[]{:S(2)}) %copy-start.1) | copy-done | bytes 131096
  3.2 0.0 copy-start.2
  3.2 0.8 %copy-done.2 = bf16[128,128]{1,0:T(8,128)(2,1)S(1)} copy-done((bf16[128,128]{1,0:T(8,128)(2,1)S(1)}, bf16[128,128]{1,0:T(8,128)(2,1)}, u32[]{:S(2)}) %copy-start.2) | copy-done | bytes 32792
  4.0 0.0 copy-start.3
  4.0 0.8 %copy-done.3 = bf16[128,128]{1,0:T(8,128)(2,1)S(1)} copy-done((bf16[128,128]{1,0:T(8,128)(2,1)S(1)}, bf16[128,128]{1,0:T(8,128)(2,1)}, u32[]{:S(2)}) %copy-start.3) | copy-done | bytes 32792
  4.8 35.6 %sparse_attention.1 = (bf16[128,512]{1,0:T(8,128)(2,1)S(1)}, bf16[128,512]{1,0:T(8,128)(2,1)S(1)}, bf16[128,128]{1,0:T(8,128)(2,1)S(1)}, bf16[128,128]{1,0:T(8,128)(2,1)S(1)}) custom-call(bf16[128,512]{1,0:T(8,128)(2,1)S(1)} %copy-done, bf16[128,128]{1,0:T(8,128)(2,1)S(1)} %copy-done.2, bf16[128,128]{1,0:T(8,128)(2,1)S(1)} %copy-done.3, ...), custom_call_target="tpu_custom_call" | custom-call | tf_op jit(solution)/shard_map/sparse_attention/pallas_call | solution.py:386
  40.4 0.7 %copy.16 = bf16[128,512]{1,0:T(8,128)(2,1)} copy(bf16[128,512]{1,0:T(8,128)(2,1)S(1)} %get-tuple-element.8) | data formatting | bytes 262144
  41.0 0.7 %copy.17 = bf16[128,512]{1,0:T(8,128)(2,1)} copy(bf16[128,512]{1,0:T(8,128)(2,1)S(1)} %get-tuple-element.9) | data formatting | bytes 262144
  41.7 0.6 %copy.18 = bf16[128,128]{1,0:T(8,128)(2,1)} copy(bf16[128,128]{1,0:T(8,128)(2,1)S(1)} %get-tuple-element.10) | data formatting | bytes 65536
  42.3 0.6 %copy.19 = bf16[128,128]{1,0:T(8,128)(2,1)} copy(bf16[128,128]{1,0:T(8,128)(2,1)S(1)} %get-tuple-element.11) | data formatting | bytes 65536
Async XLA Ops:
  0.6 0.8 %copy-start.5 = (s32[16]{0:T(128)S(1)}, s32[16]{0:T(128)}, u32[]{:S(2)}) copy-start(s32[16]{0:T(128)} %slot_ref.1) | copy-start | bytes 196
  0.6 0.8 %copy-start.4 = (s32[16]{0:T(128)S(1)}, s32[16]{0:T(128)}, u32[]{:S(2)}) copy-start(s32[16]{0:T(128)} %counts_ref.1) | copy-start | bytes 196
  1.4 0.9 %copy-start = (bf16[128,512]{1,0:T(8,128)(2,1)S(1)}, bf16[128,512]{1,0:T(8,128)(2,1)}, u32[]{:S(2)}) copy-start(bf16[128,512]{1,0:T(8,128)(2,1)} %q_ref.1) | copy-start | bytes 393220
  2.3 0.9 %copy-start.1 = (bf16[128,512]{1,0:T(8,128)(2,1)S(1)}, bf16[128,512]{1,0:T(8,128)(2,1)}, u32[]{:S(2)}) copy-start(bf16[128,512]{1,0:T(8,128)(2,1)} %g_ref.1) | copy-start | bytes 393220
  3.2 0.8 %copy-start.2 = (bf16[128,128]{1,0:T(8,128)(2,1)S(1)}, bf16[128,128]{1,0:T(8,128)(2,1)}, u32[]{:S(2)}) copy-start(bf16[128,128]{1,0:T(8,128)(2,1)} %k_ref.1) | copy-start | bytes 98308
  4.0 0.8 %copy-start.3 = (bf16[128,128]{1,0:T(8,128)(2,1)S(1)}, bf16[128,128]{1,0:T(8,128)(2,1)}, u32[]{:S(2)}) copy-start(bf16[128,128]{1,0:T(8,128)(2,1)} %v_ref.1) | copy-start | bytes 98308

commit v2 on v1

--- a/solution.py
+++ b/solution.py
@@ -36,9 +36,9 @@
 
 def kernel(
     sizes,
-    q_ref, k_ref, v_ref, g_ref, lists_ref, counts_ref, slot_ref,
+    q_hbm, k_hbm, v_hbm, g_hbm, lists_ref, counts_ref, slot_ref,
     out_ref, dq_ref, dk_ref, dv_ref,
-    kv, q_rows, g_rows, q_cols, g_cols, bias, tri, top, total, acc, dq_acc, tops,
+    q_ref, g_ref, load_sem, kv, q_rows, g_rows, q_cols, g_cols, bias, tri, top, total, acc, dq_acc, tops,
     exps, dprobs, part, from_core, from_x, from_z,
     ag_send, ag_recv, rs_send, rs_recv,
 ):
@@ -71,8 +71,17 @@
         return lax.rem(x + step, x_size)
 
     mine = 0
-    kv[mine, 0] = k_ref[...]
-    kv[mine, 1] = v_ref[...]
+    loads = [
+        pltpu.make_async_copy(source, target, load_sem.at[number])
+        for number, (source, target) in enumerate((
+            (k_hbm, kv.at[0, 0]),
+            (v_hbm, kv.at[0, 1]),
+            (q_hbm, q_ref),
+            (g_hbm, g_ref),
+        ))
+    ]
+    for load in loads:
+        load.start()
     barrier = pltpu.get_barrier_semaphore()
     for step in range(1, z_size):
         pl.semaphore_signal(barrier, inc=1, device_id=device(turn_z(step), x, c), device_id_type=MESH)
@@ -80,6 +89,8 @@
         pl.semaphore_signal(barrier, inc=1, device_id=device(z, turn_x(step), c), device_id_type=MESH)
     pl.semaphore_signal(barrier, inc=1, device_id=device(z, x, other), device_id_type=MESH)
 
+    loads[0].wait()
+    loads[1].wait()
     pl.semaphore_wait(barrier, z_size + x_size - 1)
 
     def share(block, there, where, number):
@@ -114,10 +125,12 @@
             core_base + x_step * z_size + z_step,
         )
 
+    loop(x_size - 1, lambda i: share_x(i + 1, 0).start())
     loop(z_size - 1, lambda i: share_z(i + 1).start(), 15)
-    loop(x_size - 1, lambda i: share_x(i + 1, 0).start())
     share_core(0, 0).start()
 
+    loads[2].wait()
+    loads[3].wait()
     for h in range(heads):
         cols = slice(h * head_dim, (h + 1) * head_dim)
         q_tile = q_ref[:, cols]
@@ -271,33 +284,31 @@
             place(z_step, 0, 0), from_z, z_step - 1, device(turn_z(z_step), x, c), z_step - 1
         )
 
-    def to_core(x_at):
-        def one(z_at):
-            block = place(z_at, x_at, 1)
-            post(block, backward(block))
-            give_core(x_at, z_at).start()
-
-        loop(z_size, one, 0)
-
-    def to_x(x_step):
-        x_at = x_step
-
-        def one(i):
-            z_at = lax.rem(i + 1, z_size)
-            block = place(z_at, x_at, 0)
-            pair = backward(block)
-            give_core(x_at, z_at).wait_recv()
-            post(block, plus(pair, from_core, x_at * z_size + z_at))
-            give_x(x_step, z_at).start()
-
-        loop(z_size, one, 0)
+    def one_to_core(x_at, z_at):
+        block = place(z_at, x_at, 1)
+        post(block, backward(block))
+        give_core(x_at, z_at).start()
+
+    def one_to_x(x_step, z_at):
+        block = place(z_at, x_step, 0)
+        pair = backward(block)
+        give_core(x_step, z_at).wait_recv()
+        post(block, plus(pair, from_core, x_step * z_size + z_at))
+        give_x(x_step, z_at).start()
 
     def away(i):
-        to_core(i + 1)
-        to_x(i + 1)
+        x_step = i + 1
+        one_to_core(x_step, 1 % z_size)
+
+        def both(j):
+            one_to_core(x_step, lax.rem(j + 2, z_size))
+            one_to_x(x_step, j + 1)
+
+        loop(z_size - 1, both, 0)
+        one_to_x(x_step, 0)
 
     loop(x_size - 1, away, 1)
-    to_core(0)
+    loop(z_size, lambda j: one_to_core(0, lax.rem(j + 1, z_size)), 0)
 
     def gathered(z_at, own):
         block = place(z_at, 0, 0)
@@ -352,9 +363,12 @@
             jax.ShapeDtypeStruct(keys.shape, BF16),
             jax.ShapeDtypeStruct(values.shape, BF16),
         ),
-        in_specs=[vmem] * 4 + [smem] * 3,
+        in_specs=[pl.BlockSpec(memory_space=pl.ANY)] * 4 + [smem] * 3,
         out_specs=(vmem,) * 4,
         scratch_shapes=[
+            pltpu.VMEM(queries.shape, BF16),
+            pltpu.VMEM(queries.shape, BF16),
+            pltpu.SemaphoreType.DMA((4,)),
             pltpu.VMEM((device_total, 2, BLK, head_dim), BF16),
             pltpu.VMEM((rows, head_dim), BF16),
             pltpu.VMEM((rows, head_dim), BF16),

time: 43.2 us -> 43.6 us (level)
  no operation moved by 1% of the time
where the time goes in v2:
time: 43.6 us; the launch traced here: 43.2 us
  Pallas kernels  35.9 us (82%)
  local copies, waits for them, and re-layouts  6.64 us (15%)
  between operations  0.66 us (2%)
    pallas_call x1, Pallas kernels, per_device(): call(queries, keys, values, grad_out, key_blocks, key_counts, block_slot)  35.9 us
    unnamed x17, local copies, waits for them, and re-layouts  6.64 us

profile of v2, /device:TPU:0, one launch (start us, length us, event | category | flops | bytes accessed | tf_op | source)
XLA Modules:
  0.0 43.2 jit_solution(1702723893720201183)
XLA Ops:
  0.6 0.0 copy-start.5
  0.6 0.0 copy-start.4
  0.7 0.8 %copy.11.lists_ref = s32[16,8]{1,0:T(8,128)S(1)} copy(s32[16,8]{0,1:T(8,128)} %param.11) | data formatting | bytes 1024 | tf_op args[4]
  1.4 0.0 copy-done.5
  1.4 0.0 copy-done.4
  1.4 0.0 copy-start
  1.4 0.9 %copy-done = bf16[128,512]{1,0:T(8,128)(2,1)S(1)} copy-done((bf16[128,512]{1,0:T(8,128)(2,1)S(1)}, bf16[128,512]{1,0:T(8,128)(2,1)}, u32[]{:S(2)}) %copy-start) | copy-done | bytes 131096
  2.3 0.0 copy-start.1
  2.3 0.9 %copy-done.1 = bf16[128,512]{1,0:T(8,128)(2,1)S(1)} copy-done((bf16[128,512]{1,0:T(8,128)(2,1)S(1)}, bf16[128,512]{1,0:T(8,128)(2,1)}, u32[]{:S(2)}) %copy-start.1) | copy-done | bytes 131096
  3.2 0.0 copy-start.2
  3.2 0.8 %copy-done.2 = bf16[128,128]{1,0:T(8,128)(2,1)S(1)} copy-done((bf16[128,128]{1,0:T(8,128)(2,1)S(1)}, bf16[128,128]{1,0:T(8,128)(2,1)}, u32[]{:S(2)}) %copy-start.2) | copy-done | bytes 32792
  4.0 0.0 copy-start.3
  4.0 0.8 %copy-done.3 = bf16[128,128]{1,0:T(8,128)(2,1)S(1)} copy-done((bf16[128,128]{1,0:T(8,128)(2,1)S(1)}, bf16[128,128]{1,0:T(8,128)(2,1)}, u32[]{:S(2)}) %copy-start.3) | copy-done | bytes 32792
  4.8 35.9 %sparse_attention.1 = (bf16[128,512]{1,0:T(8,128)(2,1)S(1)}, bf16[128,512]{1,0:T(8,128)(2,1)S(1)}, bf16[128,128]{1,0:T(8,128)(2,1)S(1)}, bf16[128,128]{1,0:T(8,128)(2,1)S(1)}) custom-call(bf16[128,512]{1,0:T(8,128)(2,1)S(1)} %copy-done, bf16[128,128]{1,0:T(8,128)(2,1)S(1)} %copy-done.2, bf16[128,128]{1,0:T(8,128)(2,1)S(1)} %copy-done.3, ...), custom_call_target="tpu_custom_call" | custom-call | tf_op jit(solution)/shard_map/sparse_attention/pallas_call | solution.py:400
  40.7 0.7 %copy.16 = bf16[128,512]{1,0:T(8,128)(2,1)} copy(bf16[128,512]{1,0:T(8,128)(2,1)S(1)} %get-tuple-element.8) | data formatting | bytes 262144
  41.3 0.7 %copy.17 = bf16[128,512]{1,0:T(8,128)(2,1)} copy(bf16[128,512]{1,0:T(8,128)(2,1)S(1)} %get-tuple-element.9) | data formatting | bytes 262144
  42.0 0.6 %copy.18 = bf16[128,128]{1,0:T(8,128)(2,1)} copy(bf16[128,128]{1,0:T(8,128)(2,1)S(1)} %get-tuple-element.10) | data formatting | bytes 65536
  42.6 0.6 %copy.19 = bf16[128,128]{1,0:T(8,128)(2,1)} copy(bf16[128,128]{1,0:T(8,128)(2,1)S(1)} %get-tuple-element.11) | data formatting | bytes 65536
Async XLA Ops:
  0.6 0.8 %copy-start.5 = (s32[16]{0:T(128)S(1)}, s32[16]{0:T(128)}, u32[]{:S(2)}) copy-start(s32[16]{0:T(128)} %slot_ref.1) | copy-start | bytes 196
  0.6 0.8 %copy-start.4 = (s32[16]{0:T(128)S(1)}, s32[16]{0:T(128)}, u32[]{:S(2)}) copy-start(s32[16]{0:T(128)} %counts_ref.1) | copy-start | bytes 196
  1.4 0.9 %copy-start = (bf16[128,512]{1,0:T(8,128)(2,1)S(1)}, bf16[128,512]{1,0:T(8,128)(2,1)}, u32[]{:S(2)}) copy-start(bf16[128,512]{1,0:T(8,128)(2,1)} %q_hbm.1) | copy-start | bytes 393220
  2.3 0.9 %copy-start.1 = (bf16[128,512]{1,0:T(8,128)(2,1)S(1)}, bf16[128,512]{1,0:T(8,128)(2,1)}, u32[]{:S(2)}) copy-start(bf16[128,512]{1,0:T(8,128)(2,1)} %g_hbm.1) | copy-start | bytes 393220
  3.2 0.8 %copy-start.2 = (bf16[128,128]{1,0:T(8,128)(2,1)S(1)}, bf16[128,128]{1,0:T(8,128)(2,1)}, u32[]{:S(2)}) copy-start(bf16[128,128]{1,0:T(8,128)(2,1)} %k_hbm.1) | copy-start | bytes 98308
  4.0 0.8 %copy-start.3 = (bf16[128,128]{1,0:T(8,128)(2,1)S(1)}, bf16[128,128]{1,0:T(8,128)(2,1)}, u32[]{:S(2)}) copy-start(bf16[128,128]{1,0:T(8,128)(2,1)} %v_hbm.1) | copy-start | bytes 98308

commit v3 on v2

--- a/solution.py
+++ b/solution.py
@@ -344,6 +344,18 @@
     )
 
 
+def store_kernel(*refs):
+    sources, targets, sem = refs[:4], refs[4:8], refs[8]
+    copies = [
+        pltpu.make_async_copy(source, target, sem.at[number])
+        for number, (source, target) in enumerate(zip(sources, targets))
+    ]
+    for copy in copies:
+        copy.start()
+    for copy in copies:
+        copy.wait()
+
+
 def per_device(queries, keys, values, grad_out, key_blocks, key_counts, block_slot):
     token_rows, width = queries.shape
     head_dim = keys.shape[1]
@@ -363,7 +375,7 @@
             jax.ShapeDtypeStruct(keys.shape, BF16),
             jax.ShapeDtypeStruct(values.shape, BF16),
         ),
-        in_specs=[pl.BlockSpec(memory_space=pl.ANY)] * 4 + [smem] * 3,
+        in_specs=[pl.BlockSpec(memory_space=pltpu.HBM)] * 4 + [smem] * 3,
         out_specs=(vmem,) * 4,
         scratch_shapes=[
             pltpu.VMEM(queries.shape, BF16),
@@ -393,11 +405,20 @@
             pltpu.SemaphoreType.DMA((device_total,)),
         ],
         compiler_params=pltpu.CompilerParams(
-            collective_id=0, has_side_effects=True, vmem_limit_bytes=48 * 1024 * 1024
+            collective_id=0, has_side_effects=True, vmem_limit_bytes=63 * 1024 * 1024
         ),
         name="sparse_attention",
     )
-    return call(queries, keys, values, grad_out, key_blocks, key_counts, block_slot)
+    results = call(queries, keys, values, grad_out, key_blocks, key_counts, block_slot)
+    return pl.pallas_call(
+        store_kernel,
+        out_shape=tuple(jax.ShapeDtypeStruct(r.shape, r.dtype) for r in results),
+        in_specs=[pl.BlockSpec(memory_space=pl.ANY)] * 4,
+        out_specs=(pl.BlockSpec(memory_space=pltpu.HBM),) * 4,
+        scratch_shapes=[pltpu.SemaphoreType.DMA((4,))],
+        compiler_params=pltpu.CompilerParams(vmem_limit_bytes=63 * 1024 * 1024),
+        name="store_results",
+    )(*results)
 
 
 def solution(mesh):

time: 43.6 us -> 49.7 us (1.14)
  Pallas kernels: 35.9 us -> 47.5 us
  local copies, waits for them, and re-layouts: 6.64 us -> 1.36 us
    pallas_call x0 -> x1, Pallas kernels: none -> 11.1 us  [per_device(): pl.pallas_call(store_kernel, out_shape=tuple((jax.ShapeDtypeStruct(r.shap...]
    unnamed x17 -> x1, local copies, waits for them, and re-layouts: 6.64 us -> 1.36 us
where the time goes in v3:
time: 49.7 us; the launch traced here: 49.5 us
  Pallas kernels  47.5 us (96%)
  local copies, waits for them, and re-layouts  1.36 us (3%)
  between operations  0.64 us (1%)
    pallas_call x1, Pallas kernels, per_device(): call(queries, keys, values, grad_out, key_blocks, key_counts, block_slot)  36.4 us
    pallas_call x1, Pallas kernels, per_device(): pl.pallas_call(store_kernel, out_shape=tuple((jax.ShapeDtypeStruct(r.shap...  11.1 us
    unnamed x1, local copies, waits for them, and re-layouts  1.36 us

profile of v3, /device:TPU:0, one launch (start us, length us, event | category | flops | bytes accessed | tf_op | source)
XLA Modules:
  0.0 49.5 jit_solution(8835584391366596314)
XLA Ops:
  0.6 1.4 %copy.11.lists_ref = s32[16,8]{1,0:T(8,128)} copy(s32[16,8]{0,1:T(8,128)} %param.11) | data formatting | bytes 1024 | tf_op args[4]
  2.0 36.4 %sparse_attention.1 = (bf16[128,512]{1,0:T(8,128)(2,1)}, bf16[128,512]{1,0:T(8,128)(2,1)}, bf16[128,128]{1,0:T(8,128)(2,1)}, bf16[128,128]{1,0:T(8,128)(2,1)}) custom-call(bf16[128,512]{1,0:T(8,128)(2,1)} %q_hbm.1, bf16[128,128]{1,0:T(8,128)(2,1)} %k_hbm.1, bf16[128,128]{1,0:T(8,128)(2,1)} %v_hbm.1, bf16[128,512]{1,0:T(8,128)(2,1)} %g_hbm.1, ...), custom_call_target="tpu_custom_call" | custom-call | tf_op jit(solution)/shard_map/sparse_attention/pallas_call | solution.py:412
  38.4 11.1 %store_results.1 = (bf16[128,512]{1,0:T(8,128)(2,1)}, bf16[128,512]{1,0:T(8,128)(2,1)}, bf16[128,128]{1,0:T(8,128)(2,1)}, bf16[128,128]{1,0:T(8,128)(2,1)}) custom-call(bf16[128,512]{1,0:T(8,128)(2,1)} %get-tuple-element.8.refs_0_, bf16[128,512]{1,0:T(8,128)(2,1)} %get-tuple-element.9.refs_1_, bf16[128,128]{1,0:T(8,128)(2,1)} %get-tuple-element.10.refs_2_, ...), custom_call_target="tpu_custom_call" | custom-call | tf_op jit(solution)/shard_map/store_results/pallas_call | solution.py:413

commit v4 on v3

--- a/solution.py
+++ b/solution.py
@@ -345,15 +345,8 @@
 
 
 def store_kernel(*refs):
-    sources, targets, sem = refs[:4], refs[4:8], refs[8]
-    copies = [
-        pltpu.make_async_copy(source, target, sem.at[number])
-        for number, (source, target) in enumerate(zip(sources, targets))
-    ]
-    for copy in copies:
-        copy.start()
-    for copy in copies:
-        copy.wait()
+    for source, target in zip(refs[:4], refs[4:]):
+        target[...] = source[...]
 
 
 def per_device(queries, keys, values, grad_out, key_blocks, key_counts, block_slot):
@@ -413,9 +406,8 @@
     return pl.pallas_call(
         store_kernel,
         out_shape=tuple(jax.ShapeDtypeStruct(r.shape, r.dtype) for r in results),
-        in_specs=[pl.BlockSpec(memory_space=pl.ANY)] * 4,
-        out_specs=(pl.BlockSpec(memory_space=pltpu.HBM),) * 4,
-        scratch_shapes=[pltpu.SemaphoreType.DMA((4,))],
+        in_specs=[vmem] * 4,
+        out_specs=(vmem,) * 4,
         compiler_params=pltpu.CompilerParams(vmem_limit_bytes=63 * 1024 * 1024),
         name="store_results",
     )(*results)

time: 49.7 us -> 40.3 us (0.81)
  Pallas kernels: 47.5 us -> 38.1 us
    pallas_call x1, Pallas kernels: 11.1 us -> 1.7 us  [per_device(): pl.pallas_call(store_kernel, out_shape=tuple((jax.ShapeDtypeStruct(r.shap...]
where the time goes in v4:
time: 40.3 us; the launch traced here: 40.1 us
  Pallas kernels  38.1 us (95%)
  local copies, waits for them, and re-layouts  1.36 us (3%)
  between operations  0.64 us (2%)
    pallas_call x1, Pallas kernels, per_device(): call(queries, keys, values, grad_out, key_blocks, key_counts, block_slot)  36.4 us
    pallas_call x1, Pallas kernels, per_device(): pl.pallas_call(store_kernel, out_shape=tuple((jax.ShapeDtypeStruct(r.shap...  1.7 us
    unnamed x1, local copies, waits for them, and re-layouts  1.36 us

profile of v4, /device:TPU:0, one launch (start us, length us, event | category | flops | bytes accessed | tf_op | source)
XLA Modules:
  0.0 40.1 jit_solution(12351891186555564188)
XLA Ops:
  0.6 1.4 %copy.11.lists_ref = s32[16,8]{1,0:T(8,128)} copy(s32[16,8]{0,1:T(8,128)} %param.11) | data formatting | bytes 1024 | tf_op args[4]
  2.0 36.4 %sparse_attention.1 = (bf16[128,512]{1,0:T(8,128)(2,1)}, bf16[128,512]{1,0:T(8,128)(2,1)}, bf16[128,128]{1,0:T(8,128)(2,1)}, bf16[128,128]{1,0:T(8,128)(2,1)}) custom-call(bf16[128,512]{1,0:T(8,128)(2,1)} %q_hbm.1, bf16[128,128]{1,0:T(8,128)(2,1)} %k_hbm.1, bf16[128,128]{1,0:T(8,128)(2,1)} %v_hbm.1, bf16[128,512]{1,0:T(8,128)(2,1)} %g_hbm.1, ...), custom_call_target="tpu_custom_call" | custom-call | tf_op jit(solution)/shard_map/sparse_attention/pallas_call | solution.py:405
  38.4 1.7 %store_results.1 = (bf16[128,512]{1,0:T(8,128)(2,1)}, bf16[128,512]{1,0:T(8,128)(2,1)}, bf16[128,128]{1,0:T(8,128)(2,1)}, bf16[128,128]{1,0:T(8,128)(2,1)}) custom-call(bf16[128,512]{1,0:T(8,128)(2,1)} %get-tuple-element.8.refs_0_, bf16[128,512]{1,0:T(8,128)(2,1)} %get-tuple-element.9.refs_1_, bf16[128,128]{1,0:T(8,128)(2,1)} %get-tuple-element.10.refs_2_, ...), custom_call_target="tpu_custom_call" | custom-call | tf_op jit(solution)/shard_map/store_results/pallas_call | solution.py:406
